TPU v7x, 256 devices: a whole 4x4x8 slice. The times are simulated.
256 devices in a mesh: ctx: 8 (over z), expert: 32 (over y, x, core).
Axes of the slice: x: 4, y: 4, z: 8, core: 2. Of those that a mesh axis runs over, the one named last changes fastest.
Arguments:
- tokens: bfloat16 [32, 1024, 1024], P('expert', 'ctx'), may hold values from -6 to 6
- chain_ids: int32 [32, 1024], P('expert', 'ctx'), may hold values from 0 to 7, never falling along the last dimension, each value on 1 to 256 neighbouring positions
- route_ids: int32 [32, 1024, 6], P('expert', 'ctx'), may hold values from 0 to 31, all different within a row; in each aligned block of 128 rows (0 to 127, 128 to 255, ..., all dimensions but the last counted through in order) at most 32 rows name the same one
- route_weights: float32 [32, 1024, 6], P('expert', 'ctx'), may hold values from 0.1 to 0.5
- attn_gain: float32 [1024], replicated, may hold values from 0.6 to 12
- ffn_gain: float32 [1024], replicated, may hold values from 0.1 to 1.9
- chain_bias: float32 [8], replicated, may hold values from 0.5 to 2.5
- w_qkv: bfloat16 [3, 1024, 1024], P(None, 'expert', 'ctx'), may hold values from -0.1875 to 0.1875
- w_out: bfloat16 [1024, 1024], P('ctx', 'expert'), may hold values from -0.75 to 0.75
- w_gateup: bfloat16 [32, 1024, 2816], P('expert'), may hold values from -0.1875 to 0.1875
- w_down: bfloat16 [32, 1408, 1024], P('expert'), may hold values from -0.15625 to 0.15625
Outputs:
- layer_out: bfloat16 [32, 1024, 1024], P('expert', 'ctx')
Inputs may be any that keep to these rules, and one draw needn't show every extreme that they name: `route_ids`: each residue names 6 different experts. Among the 128 residues of one device (aligned blocks of the residues in order, crop after crop), no expert is named by more than 32 of them, and in every draw some expert is named by exactly 32. `chain_ids`: chain numbers never fall along a crop; a chain spans 1 to 256 residues, and some chain exactly that many.
All inputs are finite; a program needn't handle non-finite values.
Results may differ from a plain program's by a relative error of at most 0.02.
The roundings to bfloat16 on the way count: a program that leaves them out, or rounds other values in their place, can miss the bound.
Values may be sent and summed in bfloat16 or wider, within the bound.
No kernel may reach another device: no remote copies, remote signals or barrier semaphores. Data moves between devices by JAX's collectives and lax.ppermute only.
A program may use at most 64 MiB of HBM per device.

v0:
```python
import math
import jax
import jax.numpy as jnp
from jax import lax
from jax.sharding import PartitionSpec as P


def rms_scale(values, gain):
    wide = values.astype(jnp.float32)
    return wide * lax.rsqrt(jnp.mean(wide * wide, axis=-1, keepdims=True) + 1e-05) * gain


def attend(query, key, value, chains, bias):
    length = query.shape[0]
    group = bias.shape[0]
    head_dim = query.shape[1] // group
    block = min(512, length)
    scale = 1.0 / math.sqrt(head_dim)
    keys = key.reshape(length, group, head_dim)
    values = value.reshape(length, group, head_dim)
    query_blocks = query.reshape(length // block, block, group, head_dim)
    chain_blocks = chains.reshape(length // block, block)

    def one_block(items):
        q_block, c_block = items
        scores = (
            jnp.einsum("qhd,khd->hqk", q_block, keys, preferred_element_type=jnp.float32) * scale
        )
        same = (c_block[:, None] == chains[None, :]).astype(jnp.float32)
        scores = scores + bias[:, None, None] * same[None]
        top = jnp.max(scores, axis=-1, keepdims=True)
        raised = jnp.exp(scores - top)
        probs = (raised / jnp.sum(raised, axis=-1, keepdims=True)).astype(jnp.bfloat16)
        return jnp.einsum("hqk,khd->qhd", probs, values, preferred_element_type=jnp.float32).astype(
            jnp.bfloat16
        )

    return lax.map(one_block, (query_blocks, chain_blocks)).reshape(length, group * head_dim)


def per_device(
    tokens,
    chain_ids,
    route_ids,
    route_weights,
    attn_gain,
    ffn_gain,
    chain_bias,
    w_qkv,
    w_out,
    w_gateup,
    w_down,
):
    tok = tokens.shape[1]
    width = tokens.shape[2]
    inputs = tokens[0]
    normed = rms_scale(inputs, attn_gain).astype(jnp.bfloat16)
    chains = lax.all_gather(chain_ids[0], "ctx", axis=0, tiled=True)
    groups = lax.axis_size("ctx")
    per_group = chain_bias.shape[0] // groups
    bias = lax.dynamic_slice_in_dim(chain_bias, lax.axis_index("ctx") * per_group, per_group)
    qkv_columns, out_full_rows = (
        lax.all_gather(w_qkv, "ctx", axis=2, tiled=True),
        lax.all_gather(w_out, "ctx", axis=0, tiled=True),
    )
    projected = jnp.einsum(
        "tr,ird->itd",
        normed,
        lax.all_gather(qkv_columns, "expert", axis=1, tiled=True),
        preferred_element_type=jnp.float32,
    ).astype(jnp.bfloat16)
    regrouped = lax.all_to_all(projected, "ctx", split_axis=2, concat_axis=1, tiled=True)
    attended = attend(regrouped[0], regrouped[1], regrouped[2], chains, bias)
    local_rows = lax.all_to_all(attended, "ctx", split_axis=0, concat_axis=1, tiled=True)
    mixed = inputs.astype(jnp.float32) + jnp.dot(
        local_rows,
        lax.all_gather(out_full_rows, "expert", axis=1, tiled=True),
        preferred_element_type=jnp.float32,
    )
    ffn_in = rms_scale(mixed, ffn_gain).astype(jnp.bfloat16)
    held = w_gateup.shape[0]
    experts = lax.axis_size("expert") * held
    topk = route_ids.shape[2]
    cap = min(tok, tok * topk * 4 // (experts * 3))
    hidden = w_down.shape[1]
    flat_ids = route_ids[0].reshape(-1)
    onehot = (flat_ids[:, None] == jnp.arange(experts, dtype=jnp.int32)[None, :]).astype(jnp.int32)
    rank = jnp.sum((jnp.cumsum(onehot, axis=0) - onehot) * onehot, axis=1)
    slots = flat_ids * cap + rank
    select = jnp.sum(
        (
            slots.reshape(tok, topk)[:, :, None]
            == jnp.arange(experts * cap, dtype=jnp.int32)[None, None, :]
        ).astype(jnp.bfloat16),
        axis=1,
    )
    outgoing = lax.dot_general(
        select, ffn_in, (((0,), (0,)), ((), ())), preferred_element_type=jnp.float32
    )
    outgoing = outgoing.astype(jnp.bfloat16).reshape(experts, cap, width)
    block = lax.all_to_all(outgoing, "expert", split_axis=0, concat_axis=0, tiled=True)
    count = block.shape[1]
    grouped = block.reshape(-1, held, count, width)
    both = jnp.einsum("sxcd,xdf->sxcf", grouped, w_gateup, preferred_element_type=jnp.float32)
    active = (jax.nn.silu(both[..., :hidden]) * both[..., hidden:]).astype(jnp.bfloat16)
    result = jnp.einsum(
        "sxcf,xfd->sxcd", active, w_down, preferred_element_type=jnp.float32
    ).astype(jnp.bfloat16)
    returned = lax.all_to_all(
        result.reshape(-1, count, width), "expert", split_axis=0, concat_axis=0, tiled=True
    )
    picked = jnp.take(returned.reshape(-1, width), slots, axis=0).reshape(tok, topk, width)
    weights = route_weights[0]
    moe_sum = mixed
    for route in range(topk):
        moe_sum = moe_sum + weights[:, route : route + 1] * picked[:, route].astype(jnp.float32)
    return moe_sum.astype(jnp.bfloat16)[None]


def solution(mesh):
    placed = (
        P("expert", "ctx", None),
        P("expert", "ctx"),
        P("expert", "ctx", None),
        P("expert", "ctx", None),
        P(),
        P(),
        P(),
        P(None, "expert", "ctx"),
        P("ctx", "expert"),
        P("expert", None, None),
        P("expert", None, None),
    )
    return jax.shard_map(
        per_device, mesh=mesh, in_specs=placed, out_specs=P("expert", "ctx", None), check_vma=False
    )
```

profile of v0, /device:TPU:1, one launch (start us, length us, event | category | flops | bytes accessed | tf_op | source)
XLA Modules:
  0.0 299.5 jit_solution(6906347522959631811)
XLA Ops:
  6.5 23.7 %all_gather.15 = bf16[3,32,1024]{2,1,0:T(8,128)(2,1)} all-gather(bf16[3,32,128]{2,1,0:T(8,128)(2,1)} %param.20), channel_id=1, replica_groups=mesh['ctx'=8,'expert'=32] {'ctx'}, dimensions={2}, use_global_device_ids=true | all-gather | bytes 221184 | tf_op jit(solution)/shard_map/all_gather | solution.py:63
  30.3 1.1 fusion.22
  31.4 57.7 %all-gather.4.cloned.1.call-done = bf16[3,1024,1024]{2,1,0:T(8,128)(2,1)} async-done(((bf16[3,32,1024]{2,1,0:T(8,128)(2,1)}), bf16[3,1024,1024]{2,1,0:T(8,128)(2,1)}) %all-gather.4.cloned.1.call-update) | async-done | bytes 6291472 | tf_op jit(solution)/shard_map/all_gather | solution.py:69
  89.0 4.8 %fusion.21 = bf16[3,128,1024]{2,1,0:T(8,128)(2,1)} fusion(bf16[3,1024,1024]{2,1,0:T(8,128)(2,1)} %all-gather.4.cloned.1.call-done, bf16[1,128,1024]{2,1,0:T(8,128)(2,1)} %param.13, f32[1024]{0:T(1024)} %param.17, f32[128]{0:T(128)S(1)} %add_rsqrt_fusion.1), kind=kOutput, calls=%fused_computation.28 | convolution fusion | flops 806223872 | bytes 7344640 | tf_op jit(solution)/shard_map/tr,ird->itd/dot_general | solution.py:66
  93.9 2.4 copy.69
  96.3 6.7 %all-to-all-start = ((bf16[3,128,1024]{1,0,2:T(4,128)(2,1)}), bf16[3,128,1024]{1,0,2:T(4,128)(2,1)}, u32[]{:S(2)}, u32[]{:S(2)}) async-start(bf16[3,128,1024]{1,0,2:T(4,128)(2,1)} %copy.69), calls=%async_computation | async-start | bytes 2097152 | tf_op jit(solution)/shard_map/all_to_all | solution.py:72
  103.1 39.4 %all_gather.18 = bf16[1024,32]{0,1:T(8,128)(2,1)} all-gather(bf16[128,32]{0,1:T(8,128)(2,1)S(1)} %copy-done.6), channel_id=1, replica_groups=mesh['ctx'=8,'expert'=32] {'ctx'}, dimensions={0}, use_global_device_ids=true | all-gather | bytes 73728 | tf_op jit(solution)/shard_map/all_gather | solution.py:64
  143.0 11.5 %all-gather = s32[1,1024]{1,0:T(1,128)S(1)} all-gather(s32[1,128]{1,0:T(1,128)S(1)} %copy-done.9), channel_id=2, replica_groups=mesh['ctx'=8,'expert'=32] {'ctx'}, dimensions={1}, use_global_device_ids=true | all-gather | bytes 4608 | tf_op jit(solution)/shard_map/all_gather | solution.py:58
  155.7 1.7 reduce-window.6
  158.3 1.3 copy.70
  160.5 1.8 copy.71
  162.3 0.8 copy.72
  163.1 0.8 copy.73
  164.0 8.2 %while.10 = (s32[]{:T(128)}, bf16[2,512,1,128]{3,1,2,0:T(8,128)(2,1)}, bf16[2,512,1,128]{3,1,2,0:T(8,128)(2,1)}, bf16[1024,1,128]{2,0,1:T(8,128)(2,1)}, s32[2,51...) while((s32[]{:T(128)}, ...), condition=%wide.region_4.5_spmd, body=%wide.region_1.4_spmd.sunk | while | flops 273742848 | bytes 10245305 | solution.py:38
  164.0 2.3 fusion.58
  168.1 2.3 fusion.58
  172.2 4.2 %all-to-all-start.1 = ((bf16[8,128,128]{2,1,0:T(8,128)(2,1)}), bf16[8,128,128]{2,1,0:T(8,128)(2,1)S(1)}, u32[]{:S(2)}, u32[]{:S(2)}) async-start(bf16[8,128,128]{2,1,0:T(8,128)(2,1)} %bitcast.176), calls=%async_computation.1 | async-start | bytes 524288 | tf_op jit(solution)/shard_map/all_to_all | solution.py:74
  176.8 1.1 fusion.20
  177.9 7.9 %all-to-all-done.1 = bf16[8,128,128]{2,1,0:T(8,128)(2,1)S(1)} async-done(((bf16[8,128,128]{2,1,0:T(8,128)(2,1)}), bf16[8,128,128]{2,1,0:T(8,128)(2,1)S(1)}, u32[]{:S(2)}, u32[]{:S(2)}) %all-to-all-start.1) | async-done | bytes 262176 | tf_op jit(solution)/shard_map/all_to_all | solution.py:74
  185.8 0.9 copy.75
  186.6 6.5 %all-gather.6.cloned.1.call-done = bf16[1024,1024]{0,1:T(8,128)(2,1)} async-done(((bf16[1024,32]{0,1:T(8,128)(2,1)}), bf16[1024,1024]{0,1:T(8,128)(2,1)}) %all-gather.6.cloned.1.call-update) | async-done | bytes 2097168 | tf_op jit(solution)/shard_map/all_gather | solution.py:77
  193.2 2.6 multiply_reduce_fusion
  195.8 0.8 convolution_convert_fusion.1
  196.6 37.6 %all_to_all.44 = bf16[32,32,1024]{2,1,0:T(8,128)(2,1)S(1)} all-to-all(bf16[32,32,1024]{2,1,0:T(8,128)(2,1)S(1)} %bitcast.172), channel_id=1, replica_groups=mesh['ctx'=8,'expert'=32] {'expert'}, dimensions={0} | all-to-all | bytes 4194304 | tf_op jit(solution)/shard_map/all_to_all | solution.py:101
  234.2 6.1 %convolution_bitcast_fusion = f32[32,1,32,2816]{3,2,0,1:T(8,128)S(1)} fusion(bf16[32,32,1024]{2,1,0:T(8,128)(2,1)S(1)} %all_to_all.44, bf16[1,1024,2816]{2,1,0:T(8,128)(2,1)S(1)} %copy-done.10), kind=kOutput, calls=%fused_computation.14 | convolution fusion | flops 5905580032 | bytes 19398656 | tf_op jit(solution)/shard_map/sxcd,xdf->sxcf/dot_general | solution.py:104
  240.4 4.8 %fusion.15 = bf16[32,32,1024]{2,1,0:T(8,128)(2,1)} fusion(bf16[1,1408,1024]{2,1,0:T(8,128)(2,1)S(1)} %copy-done, f32[32,1,32,2816]{3,2,0,1:T(8,128)S(1)} %convolution_bitcast_fusion), kind=kOutput, calls=%fused_computation.23 | convolution fusion | flops 2962489344 | bytes 16515072 | tf_op jit(solution)/shard_map/sxcf,xfd->sxcd/dot_general | solution.py:106
  245.2 4.9 %all-to-all-start.3 = ((bf16[32,32,1024]{2,1,0:T(8,128)(2,1)}), bf16[32,32,1024]{2,1,0:T(8,128)(2,1)}, u32[]{:S(2)}, u32[]{:S(2)}) async-start(bf16[32,32,1024]{2,1,0:T(8,128)(2,1)} %fusion.15), calls=%async_computation.3 | async-start | bytes 4194304 | tf_op jit(solution)/shard_map/all_to_all | solution.py:109
  250.4 27.6 %all-to-all-done.3 = bf16[32,32,1024]{2,1,0:T(8,128)(2,1)} async-done(((bf16[32,32,1024]{2,1,0:T(8,128)(2,1)}), bf16[32,32,1024]{2,1,0:T(8,128)(2,1)}, u32[]{:S(2)}, u32[]{:S(2)}) %all-to-all-start.3) | async-done | bytes 2097184 | tf_op jit(solution)/shard_map/all_to_all | solution.py:109
  278.0 6.4 %gather_fusion = bf16[768,1024]{1,0:T(8,128)(2,1)} fusion(bf16[1024,1024]{1,0:T(8,128)(2,1)} %bitcast.38, s32[1024]{0:T(1024)S(1)} %pad_clamp_fusion), kind=kCustom, calls=%fused_computation | custom fusion | bytes 3148800 | tf_op jit(solution)/shard_map/jit(_take)/gather | solution.py:112
  284.4 3.7 %gather.7 = bf16[128,6,1024]{2,1,0:T(8,128)(2,1)} reshape(bf16[768,1024]{1,0:T(8,128)(2,1)} %gather_fusion) | data formatting | bytes 3145728 | tf_op jit(solution)/shard_map/jit(_take)/gather | solution.py:112
  288.1 3.4 %copy_select_fusion = bf16[128,6,1024]{2,0,1:T(8,128)(2,1)S(1)} fusion(bf16[128,6,1024]{2,1,0:T(8,128)(2,1)} %gather.7, pred[128,6]{0,1:T(8,128)(4,1)S(1)} %get-tuple-element.112), kind=kLoop, calls=%fused_computation.26 | loop fusion | flops 786432 | bytes 3146496 | tf_op jit(solution)/shard_map/jit(_take)/select_n | solution.py:112
  291.6 1.1 fusion.39
  (66 shorter events, 7.6 us)
Async XLA Ops:
  6.5 233.8 %copy-start = (bf16[1,1408,1024]{2,1,0:T(8,128)(2,1)S(1)}, bf16[1,1408,1024]{2,1,0:T(8,128)(2,1)}, u32[]{:S(2)}) copy-start(bf16[1,1408,1024]{2,1,0:T(8,128)(2,1)} %param.23) | copy-start | bytes 8650756
  6.5 82.5 %all-gather.4.cloned.1.call-start = ((), (), s32[]{:S(2)}) async-start(), calls=%async_computation.4 | async-start | bytes 6488064 | tf_op jit(solution)/shard_map/all_gather | solution.py:69
  93.9 9.2 %copy-start.6 = (bf16[128,32]{0,1:T(8,128)(2,1)S(1)}, bf16[128,32]{0,1:T(8,128)(2,1)}, u32[]{:S(2)}) copy-start(bf16[128,32]{0,1:T(8,128)(2,1)} %param.21) | copy-start | bytes 24580
  93.9 48.7 %copy-start.5 = (s32[1,128,6]{1,0,2:T(1,128)S(1)}, s32[1,128,6]{1,0,2:T(1,128)}, u32[]{:S(2)}) copy-start(s32[1,128,6]{1,0,2:T(1,128)} %param.15) | copy-start | bytes 9220
  93.9 49.1 %copy-start.9 = (s32[1,128]{1,0:T(1,128)S(1)}, s32[1,128]{1,0:T(1,128)}, u32[]{:S(2)}) copy-start(s32[1,128]{1,0:T(1,128)} %param.14) | copy-start | bytes 1540
  93.9 63.8 %copy-start.11 = (f32[8]{0:T(128)S(1)}, f32[8]{0:T(128)}, u32[]{:S(2)}) copy-start(f32[8]{0:T(128)} %param.19) | copy-start | bytes 100
  96.3 62.0 %all-to-all-start = ((bf16[3,128,1024]{1,0,2:T(4,128)(2,1)}), bf16[3,128,1024]{1,0,2:T(4,128)(2,1)}, u32[]{:S(2)}, u32[]{:S(2)}) async-start(bf16[3,128,1024]{1,0,2:T(4,128)(2,1)} %copy.69), calls=%async_computation | async-start | bytes 2097152 | tf_op jit(solution)/shard_map/all_to_all | solution.py:72
  103.0 90.1 %all-gather.6.cloned.1.call-start = ((), (), s32[]{:S(2)}) async-start(), calls=%async_computation.5 | async-start | bytes 2162688 | tf_op jit(solution)/shard_map/all_gather | solution.py:77
  164.0 2.8 copy-start.2
  164.0 2.8 copy-start.4
  167.4 0.7 copy-start.3
  168.1 2.8 copy-start.2
  168.1 2.8 copy-start.4
  171.5 0.7 copy-start.3
  172.2 13.6 %all-to-all-start.1 = ((bf16[8,128,128]{2,1,0:T(8,128)(2,1)}), bf16[8,128,128]{2,1,0:T(8,128)(2,1)S(1)}, u32[]{:S(2)}, u32[]{:S(2)}) async-start(bf16[8,128,128]{2,1,0:T(8,128)(2,1)} %bitcast.176), calls=%async_computation.1 | async-start | bytes 524288 | tf_op jit(solution)/shard_map/all_to_all | solution.py:74
  176.4 19.4 %copy-start.7 = (f32[1024]{0:T(1024)S(1)}, f32[1024]{0:T(1024)}, u32[]{:S(2)}) copy-start(f32[1024]{0:T(1024)} %param.18) | copy-start | bytes 12292
  193.2 2.6 copy-start.1
  195.8 38.4 %copy-start.10 = (bf16[1,1024,2816]{2,1,0:T(8,128)(2,1)S(1)}, bf16[1,1024,2816]{2,1,0:T(8,128)(2,1)}, u32[]{:S(2)}) copy-start(bf16[1,1024,2816]{2,1,0:T(8,128)(2,1)} %param.22) | copy-start | bytes 17301508
  245.2 5.2 %copy-start.8 = (f32[1,128,6]{1,0,2:T(1,128)S(1)}, f32[1,128,6]{1,0,2:T(1,128)}, u32[]{:S(2)}) copy-start(f32[1,128,6]{1,0,2:T(1,128)} %param.16) | copy-start | bytes 9220
  245.2 32.9 %all-to-all-start.3 = ((bf16[32,32,1024]{2,1,0:T(8,128)(2,1)}), bf16[32,32,1024]{2,1,0:T(8,128)(2,1)}, u32[]{:S(2)}, u32[]{:S(2)}) async-start(bf16[32,32,1024]{2,1,0:T(8,128)(2,1)} %fusion.15), calls=%async_computation.3 | async-start | bytes 4194304 | tf_op jit(solution)/shard_map/all_to_all | solution.py:109
Sparse Core Ops, SparseCore 0:
  30.4 58.5 all-gather.3
  142.7 50.4 all-gather.5
where the time goes:
time: 300 us
  blocking collectives  112 us (37%)
  waiting for transfers between devices  99.7 us (33%)
  matrix products  24.9 us (8%)
  local copies, waits for them, and re-layouts  22.7 us (8%)
  starting transfers between devices  15.9 us (5%)
  between operations  13.6 us (5%)
  other arithmetic  10.4 us (3%)
    all_gather x1, waiting for transfers between devices, per_device(): lax.all_gather(qkv_columns, 'expert', axis=1, tiled=True)  57.7 us
    all_gather x1, blocking collectives, per_device(): lax.all_gather(w_out, 'ctx', axis=0, tiled=True)  39.4 us
    all_to_all x1, blocking collectives, per_device(): lax.all_to_all(outgoing, 'expert', split_axis=0, concat_axis=0, tiled=True)  37.6 us
    all_to_all x1, waiting for transfers between devices, per_device(): lax.all_to_all(result.reshape(-1, count, width), 'expert', split_axis=0,...  27.6 us
    all_gather x1, blocking collectives, per_device(): lax.all_gather(w_qkv, 'ctx', axis=2, tiled=True)  23.7 us
    all_gather x1, blocking collectives, per_device(): chains = lax.all_gather(chain_ids[0], 'ctx', axis=0, tiled=True)  11.5 us
    gather x2, local copies, waits for them, and re-layouts, per_device(): jnp.take(returned.reshape(-1, width), slots, axis=0)  10.1 us
    all_to_all x1, waiting for transfers between devices, per_device(): lax.all_to_all(attended, 'ctx', split_axis=0, concat_axis=1, tiled=True)  7.86 us
  transfers between devices with their start and end apart: 5, of which 4 were waited for; matrix products, arithmetic and copies ran while one was open for 7% of the time, Pallas kernels for 0%

commit v1 on v0

--- a/solution.py
+++ b/solution.py
@@ -55,7 +55,12 @@
     width = tokens.shape[2]
     inputs = tokens[0]
     normed = rms_scale(inputs, attn_gain).astype(jnp.bfloat16)
-    chains = lax.all_gather(chain_ids[0], "ctx", axis=0, tiled=True)
+    ring = [chain_ids[0]]
+    for hop in range(7):
+        ring.append(lax.ppermute(ring[-1], "ctx", [(dev, (dev + 1) % 8) for dev in range(8)]))
+    chains = jnp.roll(
+        jnp.concatenate(ring[::-1], axis=0), (lax.axis_index("ctx") + 1) * ring[0].shape[0], axis=0
+    )
     groups = lax.axis_size("ctx")
     per_group = chain_bias.shape[0] // groups
     bias = lax.dynamic_slice_in_dim(chain_bias, lax.axis_index("ctx") * per_group, per_group)

time: 300 us -> 266 us (0.89)
  blocking collectives: 112 us -> 76 us
    all_gather x1, waiting for transfers between devices: 57.7 us -> 17.4 us  [per_device(): lax.all_gather(qkv_columns, 'expert', axis=1, tiled=True)]
    all_to_all x1, waiting for transfers between devices: 0.01 us -> 29.1 us  [per_device(): lax.all_to_all(projected, 'ctx', split_axis=2, concat_axis=1, tiled=True)]
    all_gather x1, blocking collectives: 39.4 us -> 18.3 us  [per_device(): lax.all_gather(w_out, 'ctx', axis=0, tiled=True)]
    ppermute x0 -> x7, waiting for transfers between devices: none -> 16.5 us  [per_device(): lax.ppermute(ring[-1], 'ctx', [(dev, (dev + 1) % 8) for dev in range(8)])]
    all_gather x1 -> x0, blocking collectives: 11.5 us -> none  [per_device(): chains = lax.all_gather(chain_ids[0], 'ctx', axis=0, tiled=True)]
    all_gather x1, waiting for transfers between devices: 6.53 us -> 0.01 us  [per_device(): lax.all_gather(out_full_rows, 'expert', axis=1, tiled=True)]
    all_to_all x1, blocking collectives: 37.6 us -> 34 us  [per_device(): lax.all_to_all(outgoing, 'expert', split_axis=0, concat_axis=0, tiled=True)]
  transfers between devices with their start and end apart: 5 -> 12, of which waited for: 4 -> 10; matrix products, arithmetic and copies ran while one was open for 7% -> 11% of each run, Pallas kernels for 0% -> 0%
where the time goes in v1:
time: 266 us; the launch traced here: 265 us
  waiting for transfers between devices  101 us (38%)
  blocking collectives  76 us (29%)
  matrix products  24.9 us (9%)
  local copies, waits for them, and re-layouts  23.6 us (9%)
  starting transfers between devices  16.3 us (6%)
  between operations  13.7 us (5%)
  other arithmetic  9.72 us (4%)
    all_to_all x1, blocking collectives, per_device(): lax.all_to_all(outgoing, 'expert', split_axis=0, concat_axis=0, tiled=True)  34 us
    all_to_all x1, waiting for transfers between devices, per_device(): lax.all_to_all(projected, 'ctx', split_axis=2, concat_axis=1, tiled=True)  29.1 us
    all_to_all x1, waiting for transfers between devices, per_device(): lax.all_to_all(result.reshape(-1, count, width), 'expert', split_axis=0,...  27.5 us
    all_gather x1, blocking collectives, per_device(): lax.all_gather(w_qkv, 'ctx', axis=2, tiled=True)  23.7 us
    all_gather x1, blocking collectives, per_device(): lax.all_gather(w_out, 'ctx', axis=0, tiled=True)  18.3 us
    all_gather x1, waiting for transfers between devices, per_device(): lax.all_gather(qkv_columns, 'expert', axis=1, tiled=True)  17.4 us
    ppermute x7, waiting for transfers between devices, per_device(): lax.ppermute(ring[-1], 'ctx', [(dev, (dev + 1) % 8) for dev in range(8)])  16.5 us
    all_to_all x1, waiting for transfers between devices, per_device(): lax.all_to_all(attended, 'ctx', split_axis=0, concat_axis=1, tiled=True)  10.1 us
  transfers between devices with their start and end apart: 12, of which 10 were waited for; matrix products, arithmetic and copies ran while one was open for 11% of the time, Pallas kernels for 0%

profile of v1, /device:TPU:1, one launch (start us, length us, event | category | flops | bytes accessed | tf_op | source)
XLA Modules:
  0.0 264.9 jit_solution(4581305023026038935)
XLA Ops:
  6.5 23.7 %all_gather.12 = bf16[3,32,1024]{2,1,0:T(8,128)(2,1)} all-gather(bf16[3,32,128]{2,1,0:T(8,128)(2,1)} %param.20), channel_id=1, replica_groups=mesh['ctx'=8,'expert'=32] {'ctx'}, dimensions={2}, use_global_device_ids=true | all-gather | bytes 221184 | tf_op jit(solution)/shard_map/all_gather | solution.py:68
  30.4 18.3 %all_gather.14 = bf16[1024,32]{0,1:T(8,128)(2,1)} all-gather(bf16[128,32]{0,1:T(8,128)(2,1)} %param.21), channel_id=1, replica_groups=mesh['ctx'=8,'expert'=32] {'ctx'}, dimensions={0}, use_global_device_ids=true | all-gather | bytes 73728 | tf_op jit(solution)/shard_map/all_gather | solution.py:69
  51.7 1.7 collective-permute-done.1
  53.4 1.7 reduce-window.6
  55.2 2.0 collective-permute-done.2
  57.5 3.3 %collective-permute-done.3 = s32[128]{0:T(128)S(1)} collective-permute-done((s32[128]{0:T(128)S(1)}, s32[128]{0:T(128)S(1)}, u32[]{:S(2)}, u32[]{:S(2)}) %collective-permute-start.3) | collective-permute-done | bytes 544 | tf_op jit(solution)/shard_map/ppermute | solution.py:60
  60.8 3.6 %collective-permute-done.4 = s32[128]{0:T(128)S(1)} collective-permute-done((s32[128]{0:T(128)S(1)}, s32[128]{0:T(128)S(1)}, u32[]{:S(2)}, u32[]{:S(2)}) %collective-permute-start.4) | collective-permute-done | bytes 544 | tf_op jit(solution)/shard_map/ppermute | solution.py:60
  64.6 3.4 %collective-permute-done.5 = s32[128]{0:T(128)S(1)} collective-permute-done((s32[128]{0:T(128)S(1)}, s32[128]{0:T(128)S(1)}, u32[]{:S(2)}, u32[]{:S(2)}) %collective-permute-start.5) | collective-permute-done | bytes 544 | tf_op jit(solution)/shard_map/ppermute | solution.py:60
  68.1 1.3 dynamic_slice.16
  69.3 2.3 collective-permute-done.6
  71.7 17.4 %all-gather.3.cloned.1.call-done = bf16[3,1024,1024]{2,1,0:T(8,128)(2,1)} async-done(((bf16[3,32,1024]{2,1,0:T(8,128)(2,1)}), bf16[3,1024,1024]{2,1,0:T(8,128)(2,1)}) %all-gather.3.cloned.1.call-update) | async-done | bytes 6291472 | tf_op jit(solution)/shard_map/all_gather | solution.py:74
  89.0 4.9 %fusion.21 = bf16[3,128,1024]{2,1,0:T(8,128)(2,1)} fusion(bf16[3,1024,1024]{2,1,0:T(8,128)(2,1)} %all-gather.3.cloned.1.call-done, bf16[1,128,1024]{2,1,0:T(8,128)(2,1)} %param.13, f32[1024]{0:T(1024)} %param.17, f32[128]{0:T(128)S(1)} %add_rsqrt_fusion.1), kind=kOutput, calls=%fused_computation.28 | convolution fusion | flops 806223872 | bytes 7344640 | tf_op jit(solution)/shard_map/tr,ird->itd/dot_general | solution.py:71
  93.9 2.4 copy.69
  96.3 6.7 %all-to-all-start = ((bf16[3,128,1024]{1,0,2:T(4,128)(2,1)}), bf16[3,128,1024]{1,0,2:T(4,128)(2,1)}, u32[]{:S(2)}, u32[]{:S(2)}) async-start(bf16[3,128,1024]{1,0,2:T(4,128)(2,1)} %copy.69), calls=%async_computation | async-start | bytes 2097152 | tf_op jit(solution)/shard_map/all_to_all | solution.py:77
  103.3 29.1 %all-to-all-done = bf16[3,128,1024]{1,0,2:T(4,128)(2,1)} async-done(((bf16[3,128,1024]{1,0,2:T(4,128)(2,1)}), bf16[3,128,1024]{1,0,2:T(4,128)(2,1)}, u32[]{:S(2)}, u32[]{:S(2)}) %all-to-all-start) | async-done | bytes 786464 | tf_op jit(solution)/shard_map/all_to_all | solution.py:77
  132.4 1.3 copy.70
  134.5 1.8 copy.71
  138.0 8.3 %while.10 = (s32[]{:T(128)}, bf16[2,512,1,128]{3,1,2,0:T(8,128)(2,1)}, bf16[2,512,1,128]{3,1,2,0:T(8,128)(2,1)}, bf16[1024,1,128]{2,0,1:T(8,128)(2,1)}, s32[2,51...) while((s32[]{:T(128)}, ...), condition=%wide.region_4.5_spmd, body=%wide.region_1.4_spmd.sunk | while | flops 273742848 | bytes 10245305 | solution.py:38
  138.0 2.3 fusion.58
  142.2 2.3 fusion.58
  146.3 3.6 %all-to-all-start.1 = ((bf16[8,128,128]{2,1,0:T(8,128)(2,1)}), bf16[8,128,128]{2,1,0:T(8,128)(2,1)S(1)}, u32[]{:S(2)}, u32[]{:S(2)}) async-start(bf16[8,128,128]{2,1,0:T(8,128)(2,1)} %bitcast.178), calls=%async_computation.1 | async-start | bytes 524288 | tf_op jit(solution)/shard_map/all_to_all | solution.py:79
  150.2 1.1 fusion.20
  151.4 10.1 %all-to-all-done.1 = bf16[8,128,128]{2,1,0:T(8,128)(2,1)S(1)} async-done(((bf16[8,128,128]{2,1,0:T(8,128)(2,1)}), bf16[8,128,128]{2,1,0:T(8,128)(2,1)S(1)}, u32[]{:S(2)}, u32[]{:S(2)}) %all-to-all-start.1) | async-done | bytes 262176 | tf_op jit(solution)/shard_map/all_to_all | solution.py:79
  162.3 2.6 multiply_reduce_fusion
  165.8 34.0 %all_to_all.44 = bf16[32,32,1024]{2,1,0:T(8,128)(2,1)S(1)} all-to-all(bf16[32,32,1024]{2,1,0:T(8,128)(2,1)S(1)} %bitcast.174), channel_id=1, replica_groups=mesh['ctx'=8,'expert'=32] {'expert'}, dimensions={0} | all-to-all | bytes 4194304 | tf_op jit(solution)/shard_map/all_to_all | solution.py:106
  199.8 6.1 %convolution_bitcast_fusion = f32[32,1,32,2816]{3,2,0,1:T(8,128)S(1)} fusion(bf16[32,32,1024]{2,1,0:T(8,128)(2,1)S(1)} %all_to_all.44, bf16[1,1024,2816]{2,1,0:T(8,128)(2,1)S(1)} %copy-done.8), kind=kOutput, calls=%fused_computation.14 | convolution fusion | flops 5905580032 | bytes 19398656 | tf_op jit(solution)/shard_map/sxcd,xdf->sxcf/dot_general | solution.py:109
  205.9 4.8 %fusion.15 = bf16[32,32,1024]{2,1,0:T(8,128)(2,1)} fusion(bf16[1,1408,1024]{2,1,0:T(8,128)(2,1)S(1)} %copy-done, f32[32,1,32,2816]{3,2,0,1:T(8,128)S(1)} %convolution_bitcast_fusion), kind=kOutput, calls=%fused_computation.23 | convolution fusion | flops 2962489344 | bytes 16515072 | tf_op jit(solution)/shard_map/sxcf,xfd->sxcd/dot_general | solution.py:111
  210.7 4.9 %all-to-all-start.3 = ((bf16[32,32,1024]{2,1,0:T(8,128)(2,1)}), bf16[32,32,1024]{2,1,0:T(8,128)(2,1)}, u32[]{:S(2)}, u32[]{:S(2)}) async-start(bf16[32,32,1024]{2,1,0:T(8,128)(2,1)} %fusion.15), calls=%async_computation.3 | async-start | bytes 4194304 | tf_op jit(solution)/shard_map/all_to_all | solution.py:114
  216.0 27.5 %all-to-all-done.3 = bf16[32,32,1024]{2,1,0:T(8,128)(2,1)} async-done(((bf16[32,32,1024]{2,1,0:T(8,128)(2,1)}), bf16[32,32,1024]{2,1,0:T(8,128)(2,1)}, u32[]{:S(2)}, u32[]{:S(2)}) %all-to-all-start.3) | async-done | bytes 2097184 | tf_op jit(solution)/shard_map/all_to_all | solution.py:114
  243.5 6.4 %gather_fusion = bf16[768,1024]{1,0:T(8,128)(2,1)} fusion(bf16[1024,1024]{1,0:T(8,128)(2,1)} %bitcast.38, s32[1024]{0:T(1024)S(1)} %pad_clamp_fusion), kind=kCustom, calls=%fused_computation | custom fusion | bytes 3148800 | tf_op jit(solution)/shard_map/jit(_take)/gather | solution.py:117
  249.9 3.7 %gather.7 = bf16[128,6,1024]{2,1,0:T(8,128)(2,1)} reshape(bf16[768,1024]{1,0:T(8,128)(2,1)} %gather_fusion) | data formatting | bytes 3145728 | tf_op jit(solution)/shard_map/jit(_take)/gather | solution.py:117
  253.5 3.4 %copy_select_fusion = bf16[128,6,1024]{2,0,1:T(8,128)(2,1)S(1)} fusion(bf16[128,6,1024]{2,1,0:T(8,128)(2,1)} %gather.7, pred[128,6]{0,1:T(8,128)(4,1)S(1)} %get-tuple-element.112), kind=kLoop, calls=%fused_computation.26 | loop fusion | flops 786432 | bytes 3146496 | tf_op jit(solution)/shard_map/jit(_take)/select_n | solution.py:117
  (91 shorter events, 13.2 us)
Async XLA Ops:
  6.5 199.4 %copy-start = (bf16[1,1408,1024]{2,1,0:T(8,128)(2,1)S(1)}, bf16[1,1408,1024]{2,1,0:T(8,128)(2,1)}, u32[]{:S(2)}) copy-start(bf16[1,1408,1024]{2,1,0:T(8,128)(2,1)} %param.23) | copy-start | bytes 8650756
  6.5 82.5 %all-gather.3.cloned.1.call-start = ((), (), s32[]{:S(2)}) async-start(), calls=%async_computation.4 | async-start | bytes 6488064 | tf_op jit(solution)/shard_map/all_gather | solution.py:74
  30.3 132.1 %all-gather.5.cloned.1.call-start = ((), (), s32[]{:S(2)}) async-start(), calls=%async_computation.5 | async-start | bytes 2162688 | tf_op jit(solution)/shard_map/all_gather | solution.py:82
  30.3 19.4 %collective-permute-start = (s32[128]{0:T(128)}, s32[128]{0:T(128)S(1)}, u32[]{:S(2)}, u32[]{:S(2)}) collective-permute-start(s32[128]{0:T(128)} %bitcast.185), channel_id=1, source_target_pairs={{0,32},{32,64},{64,96},{96,128},{128,160},{160,192},{192,224},{224... | collective-permute-start | bytes 1544 | tf_op jit(solution)/shard_map/ppermute | solution.py:60
  49.7 3.7 %collective-permute-start.1 = (s32[128]{0:T(128)S(1)}, s32[128]{0:T(128)S(1)}, u32[]{:S(2)}, u32[]{:S(2)}) collective-permute-start(s32[128]{0:T(128)S(1)} %collective-permute-done), channel_id=1, source_target_pairs={{0,32},{32,64},{64,96},{96,128},{128,160},{160,192},{192,224},{224... | collective-permute-start | bytes 1544 | tf_op jit(solution)/shard_map/ppermute | solution.py:60
  53.4 3.8 %collective-permute-start.2 = (s32[128]{0:T(128)S(1)}, s32[128]{0:T(128)S(1)}, u32[]{:S(2)}, u32[]{:S(2)}) collective-permute-start(s32[128]{0:T(128)S(1)} %collective-permute-done.1), channel_id=1, source_target_pairs={{0,32},{32,64},{64,96},{96,128},{128,160},{160,192},{192,224},{224... | collective-permute-start | bytes 1544 | tf_op jit(solution)/shard_map/ppermute | solution.py:60
  57.2 3.6 %collective-permute-start.3 = (s32[128]{0:T(128)S(1)}, s32[128]{0:T(128)S(1)}, u32[]{:S(2)}, u32[]{:S(2)}) collective-permute-start(s32[128]{0:T(128)S(1)} %collective-permute-done.2), channel_id=1, source_target_pairs={{0,32},{32,64},{64,96},{96,128},{128,160},{160,192},{192,224},{224... | collective-permute-start | bytes 1544 | tf_op jit(solution)/shard_map/ppermute | solution.py:60
  60.8 3.6 %collective-permute-start.4 = (s32[128]{0:T(128)S(1)}, s32[128]{0:T(128)S(1)}, u32[]{:S(2)}, u32[]{:S(2)}) collective-permute-start(s32[128]{0:T(128)S(1)} %collective-permute-done.3), channel_id=1, source_target_pairs={{0,32},{32,64},{64,96},{96,128},{128,160},{160,192},{192,224},{224... | collective-permute-start | bytes 1544 | tf_op jit(solution)/shard_map/ppermute | solution.py:60
  64.4 3.6 %collective-permute-start.5 = (s32[128]{0:T(128)S(1)}, s32[128]{0:T(128)S(1)}, u32[]{:S(2)}, u32[]{:S(2)}) collective-permute-start(s32[128]{0:T(128)S(1)} %collective-permute-done.4), channel_id=1, source_target_pairs={{0,32},{32,64},{64,96},{96,128},{128,160},{160,192},{192,224},{224... | collective-permute-start | bytes 1544 | tf_op jit(solution)/shard_map/ppermute | solution.py:60
  68.0 3.6 %collective-permute-start.6 = (s32[128]{0:T(128)S(1)}, s32[128]{0:T(128)S(1)}, u32[]{:S(2)}, u32[]{:S(2)}) collective-permute-start(s32[128]{0:T(128)S(1)} %collective-permute-done.5), channel_id=1, source_target_pairs={{0,32},{32,64},{64,96},{96,128},{128,160},{160,192},{192,224},{224... | collective-permute-start | bytes 1544 | tf_op jit(solution)/shard_map/ppermute | solution.py:60
  93.9 9.1 %copy-start.9 = (s32[1,128]{1,0:T(1,128)S(1)}, s32[1,128]{1,0:T(1,128)}, u32[]{:S(2)}) copy-start(s32[1,128]{1,0:T(1,128)} %param.14) | copy-start | bytes 1540
  96.3 36.1 %all-to-all-start = ((bf16[3,128,1024]{1,0,2:T(4,128)(2,1)}), bf16[3,128,1024]{1,0,2:T(4,128)(2,1)}, u32[]{:S(2)}, u32[]{:S(2)}) async-start(bf16[3,128,1024]{1,0,2:T(4,128)(2,1)} %copy.69), calls=%async_computation | async-start | bytes 2097152 | tf_op jit(solution)/shard_map/all_to_all | solution.py:77
  138.0 12.2 %copy-start.5 = (s32[1,128,6]{1,0,2:T(1,128)S(1)}, s32[1,128,6]{1,0,2:T(1,128)}, u32[]{:S(2)}) copy-start(s32[1,128,6]{1,0,2:T(1,128)} %param.15) | copy-start | bytes 9220
  138.0 2.8 %copy-start.2 = (bf16[2,512,1,128]{3,1,2,0:T(8,128)(2,1)S(1)}, bf16[2,512,1,128]{3,1,2,0:T(8,128)(2,1)}, u32[]{:S(2)}) copy-start(bf16[2,512,1,128]{3,1,2,0:T(8,128)(2,1)} %get-tuple-element.190) | copy-start | bytes 786436 | tf_op jit(solution)/shard_map/while
  138.0 2.8 %copy-start.4 = (bf16[1024,1,128]{2,0,1:T(8,128)(2,1)S(1)}, bf16[1024,1,128]{2,0,1:T(8,128)(2,1)}, u32[]{:S(2)}) copy-start(bf16[1024,1,128]{2,0,1:T(8,128)(2,1)} %get-tuple-element.205) | copy-start | bytes 786436 | tf_op jit(solution)/shard_map/while
  141.4 0.7 copy-start.3
  142.1 2.8 %copy-start.2 = (bf16[2,512,1,128]{3,1,2,0:T(8,128)(2,1)S(1)}, bf16[2,512,1,128]{3,1,2,0:T(8,128)(2,1)}, u32[]{:S(2)}) copy-start(bf16[2,512,1,128]{3,1,2,0:T(8,128)(2,1)} %get-tuple-element.190) | copy-start | bytes 786436 | tf_op jit(solution)/shard_map/while
  142.1 2.8 %copy-start.4 = (bf16[1024,1,128]{2,0,1:T(8,128)(2,1)S(1)}, bf16[1024,1,128]{2,0,1:T(8,128)(2,1)}, u32[]{:S(2)}) copy-start(bf16[1024,1,128]{2,0,1:T(8,128)(2,1)} %get-tuple-element.205) | copy-start | bytes 786436 | tf_op jit(solution)/shard_map/while
  145.6 0.7 copy-start.3
  146.3 15.2 %all-to-all-start.1 = ((bf16[8,128,128]{2,1,0:T(8,128)(2,1)}), bf16[8,128,128]{2,1,0:T(8,128)(2,1)S(1)}, u32[]{:S(2)}, u32[]{:S(2)}) async-start(bf16[8,128,128]{2,1,0:T(8,128)(2,1)} %bitcast.178), calls=%async_computation.1 | async-start | bytes 524288 | tf_op jit(solution)/shard_map/all_to_all | solution.py:79
  149.9 15.1 %copy-start.6 = (f32[1024]{0:T(1024)S(1)}, f32[1024]{0:T(1024)}, u32[]{:S(2)}) copy-start(f32[1024]{0:T(1024)} %param.18) | copy-start | bytes 12292
  162.3 2.6 copy-start.1
  165.0 34.8 %copy-start.8 = (bf16[1,1024,2816]{2,1,0:T(8,128)(2,1)S(1)}, bf16[1,1024,2816]{2,1,0:T(8,128)(2,1)}, u32[]{:S(2)}) copy-start(bf16[1,1024,2816]{2,1,0:T(8,128)(2,1)} %param.22) | copy-start | bytes 17301508
  210.7 5.2 %copy-start.7 = (f32[1,128,6]{1,0,2:T(1,128)S(1)}, f32[1,128,6]{1,0,2:T(1,128)}, u32[]{:S(2)}) copy-start(f32[1,128,6]{1,0,2:T(1,128)} %param.16) | copy-start | bytes 9220
  210.7 32.7 %all-to-all-start.3 = ((bf16[32,32,1024]{2,1,0:T(8,128)(2,1)}), bf16[32,32,1024]{2,1,0:T(8,128)(2,1)}, u32[]{:S(2)}, u32[]{:S(2)}) async-start(bf16[32,32,1024]{2,1,0:T(8,128)(2,1)} %fusion.15), calls=%async_computation.3 | async-start | bytes 4194304 | tf_op jit(solution)/shard_map/all_to_all | solution.py:114
Sparse Core Ops, SparseCore 0:
  30.4 58.6 all-gather.2
  91.6 47.7 all-gather.4
